TPU v7x, 32 devices: a whole 2x2x4 slice. The times are simulated.
32 devices in a mesh: dp: 8 (over y, x, core), seq: 4 (over z).
Axes of the slice: x: 2, y: 2, z: 4, core: 2. Of those that a mesh axis runs over, the one named last changes fastest.
Arguments:
- inputs: bfloat16 [32768, 768], P(('dp', 'seq')), may hold values from -6 to 6
- attn_gain: bfloat16 [768], P('dp'), may hold values from 0.25 to 1.75
- qkv_weight: bfloat16 [768, 2304], P('dp'), may hold values from -0.25 to 0.25
- proj_weight: bfloat16 [768, 768], P('dp'), may hold values from -0.4375 to 0.4375
- mlp_gain: bfloat16 [768], P('dp'), may hold values from 0.25 to 1.75
- in_weight: bfloat16 [768, 2304], P('dp'), may hold values from -0.21875 to 0.21875
- out_weight: bfloat16 [1152, 768], P('dp'), may hold values from -0.25 to 0.25
- cotangent: bfloat16 [32768, 768], P(('dp', 'seq')), may hold values from -12 to 12
Outputs:
- output: bfloat16 [32768, 768], P(('dp', 'seq'))
- input_grad: bfloat16 [32768, 768], P(('dp', 'seq'))
- attn_gain_grad: float32 [768], P('dp')
- qkv_weight_grad: float32 [768, 2304], P('dp')
- proj_weight_grad: float32 [768, 768], P('dp')
- mlp_gain_grad: float32 [768], P('dp')
- in_weight_grad: float32 [768, 2304], P('dp')
- out_weight_grad: float32 [1152, 768], P('dp')
All inputs are finite; a program needn't handle non-finite values.
Results may differ from a plain program's by a relative error of at most 0.02.
Values may be sent and summed in bfloat16 or wider, within the bound.
A program may use at most 128 MiB of HBM per device.

v0:
```python
import jax
import jax.numpy as jnp
from jax import lax
from jax.sharding import PartitionSpec as P

D = 768
HEADS = 12
HEAD_DIM = 64
FF = 1152
WINDOW = 64
QBLOCK = 512
epsilon = 1e-05
theta_base = 10000.0
masked_score = -1e30


def layer_norm(features, gain_vector):
    center = features - jnp.mean(features, -1, keepdims=True)
    spread = jnp.mean(center * center, -1, keepdims=True)
    return center * lax.rsqrt(spread + epsilon) * gain_vector


def rotary_tables(positions, head_width):
    half_width = head_width // 2
    inverse_freq = theta_base ** (-(jnp.arange(half_width, dtype=jnp.float32) * 2.0) / head_width)
    angles = positions[:, None] * inverse_freq[None, :]
    cosine_table = jnp.concatenate([jnp.cos(angles), jnp.cos(angles)], -1)
    sine_table = jnp.concatenate([jnp.sin(angles), jnp.sin(angles)], -1)
    return (cosine_table[:, None, :], sine_table[:, None, :])


def rotate(features, cosine_table, sine_table):
    half_width = features.shape[-1] // 2
    turned = jnp.concatenate([-features[..., half_width:], features[..., :half_width]], -1)
    return features * cosine_table + turned * sine_table


def gated_gelu(up_values):
    gelu_input = up_values[:, :FF]
    gate_half = up_values[:, FF:]
    return jax.nn.gelu(gelu_input, approximate=False) * gate_half


def band_scores(query_block, key_block, first_row, seq_total):
    score_scale = query_block.shape[-1] ** (-0.5)
    key_span = key_block.shape[0]
    scores = (
        jnp.einsum("qhd,khd->hqk", query_block, key_block, preferred_element_type=jnp.float32)
        * score_scale
    )
    query_pos = first_row + jnp.arange(QBLOCK, dtype=jnp.int32)[:, None]
    key_pos = first_row - WINDOW + jnp.arange(key_span, dtype=jnp.int32)[None, :]
    in_band = (jnp.abs(query_pos - key_pos) <= WINDOW) & (key_pos >= 0) & (key_pos < seq_total)
    return jnp.where(in_band[None], scores, masked_score)


def band_forward(queries, key_pad, value_pad, offset, seq_total):
    row_count = queries.shape[0]
    key_span = QBLOCK + 2 * WINDOW

    def one_block(block_index):
        row_start = block_index * QBLOCK
        query_block = lax.dynamic_slice_in_dim(queries, row_start, QBLOCK, 0)
        key_block = lax.dynamic_slice_in_dim(key_pad, row_start, key_span, 0)
        value_block = lax.dynamic_slice_in_dim(value_pad, row_start, key_span, 0)
        scores = band_scores(query_block, key_block, offset + row_start, seq_total)
        row_max = jnp.max(scores, -1, keepdims=True)
        weights = jnp.exp(scores - row_max)
        row_sum = jnp.sum(weights, -1, keepdims=True)
        softmax_low = (weights / row_sum).astype(jnp.bfloat16)
        result = jnp.einsum(
            "hqk,khd->qhd", softmax_low, value_block, preferred_element_type=jnp.float32
        )
        log_sum = jnp.transpose((row_max + jnp.log(row_sum))[:, :, 0])
        return (result, log_sum)

    results, log_sums = lax.map(one_block, jnp.arange(row_count // QBLOCK, dtype=jnp.int32))
    return (results.reshape(queries.shape), log_sums.reshape(row_count, queries.shape[1]))


def band_backward(queries, key_pad, value_pad, grad_out, log_sums, offset, seq_total):
    row_count = queries.shape[0]
    key_span = QBLOCK + 2 * WINDOW
    score_scale = queries.shape[-1] ** (-0.5)

    def one_block(carried, block_index):
        key_grads, value_grads = carried
        row_start = block_index * QBLOCK
        query_block = lax.dynamic_slice_in_dim(queries, row_start, QBLOCK, 0)
        key_block = lax.dynamic_slice_in_dim(key_pad, row_start, key_span, 0)
        value_block = lax.dynamic_slice_in_dim(value_pad, row_start, key_span, 0)
        grad_block = lax.dynamic_slice_in_dim(grad_out, row_start, QBLOCK, 0)
        lse_block = lax.dynamic_slice_in_dim(log_sums, row_start, QBLOCK, 0)
        scores = band_scores(query_block, key_block, offset + row_start, seq_total)
        softmax_out = jnp.exp(scores - jnp.transpose(lse_block)[:, :, None])
        grad_probs = jnp.einsum(
            "qhd,khd->hqk", grad_block, value_block, preferred_element_type=jnp.float32
        )
        inner_sum = jnp.sum(softmax_out * grad_probs, -1, keepdims=True)
        grad_scores = (softmax_out * (grad_probs - inner_sum)).astype(jnp.bfloat16)
        query_grad = (
            jnp.einsum("hqk,khd->qhd", grad_scores, key_block, preferred_element_type=jnp.float32)
            * score_scale
        )
        key_part = (
            jnp.einsum("hqk,qhd->khd", grad_scores, query_block, preferred_element_type=jnp.float32)
            * score_scale
        )
        value_part = jnp.einsum(
            "hqk,qhd->khd",
            softmax_out.astype(jnp.bfloat16),
            grad_block,
            preferred_element_type=jnp.float32,
        )
        key_grads = lax.dynamic_update_slice_in_dim(
            key_grads,
            lax.dynamic_slice_in_dim(key_grads, row_start, key_span, 0) + key_part,
            row_start,
            0,
        )
        value_grads = lax.dynamic_update_slice_in_dim(
            value_grads,
            lax.dynamic_slice_in_dim(value_grads, row_start, key_span, 0) + value_part,
            row_start,
            0,
        )
        return ((key_grads, value_grads), query_grad)

    padded_zero = jnp.zeros(key_pad.shape, jnp.float32)
    carried, query_grads = lax.scan(
        one_block, (padded_zero, padded_zero), jnp.arange(row_count // QBLOCK, dtype=jnp.int32)
    )
    return (query_grads.reshape(queries.shape), carried[0], carried[1])


def shards(inputs, attn_gain, qkv_weight, proj_weight, mlp_gain, in_weight, out_weight, cotangent):
    gathered = (
        lax.all_gather(qkv_weight, "dp", axis=0, tiled=True),
        lax.all_gather(proj_weight, "dp", axis=0, tiled=True),
        lax.all_gather(in_weight, "dp", axis=0, tiled=True),
        lax.all_gather(out_weight, "dp", axis=0, tiled=True),
        lax.all_gather(attn_gain, "dp", axis=0, tiled=True),
        lax.all_gather(mlp_gain, "dp", axis=0, tiled=True),
    )
    qkv_full, proj_full, in_full, out_full, attn_full, mlp_full = gathered
    tokens = inputs.shape[0]
    seq_count = lax.axis_size("seq")
    seq_total = tokens * seq_count
    offset = lax.axis_index("seq") * tokens
    local_heads = HEADS // seq_count
    residual = inputs.astype(jnp.float32)
    normed_one, norm_one_back = jax.vjp(layer_norm, residual, attn_full.astype(jnp.float32))
    normed_low = normed_one.astype(jnp.bfloat16)
    projected = jnp.dot(normed_low, qkv_full, preferred_element_type=jnp.float32)
    positions = (offset + jnp.arange(tokens, dtype=jnp.int32)).astype(jnp.float32)
    cosine_table, sine_table = rotary_tables(positions, HEAD_DIM)

    def turn_pair(raw_pairs):
        return rotate(raw_pairs.reshape(tokens, 2 * HEADS, HEAD_DIM), cosine_table, sine_table)

    turned, turn_back = jax.vjp(turn_pair, projected[:, : 2 * D])
    query_low = turned[:, :HEADS].reshape(tokens, D).astype(jnp.bfloat16)
    key_low = turned[:, HEADS:].reshape(tokens, D).astype(jnp.bfloat16)
    value_low = projected[:, 2 * D :].astype(jnp.bfloat16)
    stacked = jnp.stack([query_low, key_low, value_low], 1)
    by_heads = lax.all_to_all(stacked, "seq", split_axis=2, concat_axis=0, tiled=True)
    head_queries = by_heads[:, 0].reshape(seq_total, local_heads, HEAD_DIM)
    keys_padded = jnp.pad(
        by_heads[:, 1].reshape(seq_total, local_heads, HEAD_DIM), ((WINDOW, WINDOW), (0, 0), (0, 0))
    )
    values_padded = jnp.pad(
        by_heads[:, 2].reshape(seq_total, local_heads, HEAD_DIM), ((WINDOW, WINDOW), (0, 0), (0, 0))
    )
    attended, log_sums = band_forward(head_queries, keys_padded, values_padded, 0, seq_total)
    attended_low = attended.astype(jnp.bfloat16).reshape(seq_total, D // seq_count)
    mixed_low = lax.all_to_all(attended_low, "seq", split_axis=0, concat_axis=1, tiled=True)
    attn_out = jnp.dot(mixed_low, proj_full, preferred_element_type=jnp.float32)
    hidden_state = residual + attn_out
    normed_two, norm_two_back = jax.vjp(layer_norm, hidden_state, mlp_full.astype(jnp.float32))
    normed_two_low = normed_two.astype(jnp.bfloat16)
    up_values = jnp.dot(normed_two_low, in_full, preferred_element_type=jnp.float32)
    gated, gated_back = jax.vjp(gated_gelu, up_values)
    gated_low = gated.astype(jnp.bfloat16)
    result = hidden_state + jnp.dot(gated_low, out_full, preferred_element_type=jnp.float32)
    output = result.astype(jnp.bfloat16)
    grad_result = cotangent.astype(jnp.float32)
    out_grad = jnp.einsum("tf,td->fd", gated_low, cotangent, preferred_element_type=jnp.float32)
    gated_grad = jnp.einsum("td,fd->tf", cotangent, out_full, preferred_element_type=jnp.float32)
    up_grad = gated_back(gated_grad)[0]
    up_low = up_grad.astype(jnp.bfloat16)
    in_grad = jnp.einsum("td,tf->df", normed_two_low, up_low, preferred_element_type=jnp.float32)
    normed_two_grad = jnp.einsum("tf,df->td", up_low, in_full, preferred_element_type=jnp.float32)
    hidden_part, mlp_gain_grad = norm_two_back(normed_two_grad)
    hidden_grad = grad_result + hidden_part
    attn_low = hidden_grad.astype(jnp.bfloat16)
    proj_grad = jnp.einsum("te,td->ed", mixed_low, attn_low, preferred_element_type=jnp.float32)
    mixed_grad = jnp.einsum(
        "td,ed->te", attn_low, proj_full, preferred_element_type=jnp.float32
    ).astype(jnp.bfloat16)
    grad_heads = lax.all_to_all(mixed_grad, "seq", split_axis=1, concat_axis=0, tiled=True)
    grad_heads = grad_heads.reshape(seq_total, local_heads, HEAD_DIM)
    query_grad, key_pad_grad, value_pad_grad = band_backward(
        head_queries, keys_padded, values_padded, grad_heads, log_sums, 0, seq_total
    )
    head_grads = jnp.stack(
        [
            query_grad.reshape(seq_total, D // seq_count),
            key_pad_grad[WINDOW : WINDOW + seq_total].reshape(seq_total, D // seq_count),
            value_pad_grad[WINDOW : WINDOW + seq_total].reshape(seq_total, D // seq_count),
        ],
        1,
    ).astype(jnp.bfloat16)
    token_grads = lax.all_to_all(head_grads, "seq", split_axis=0, concat_axis=2, tiled=True)
    rotated_grad = jnp.concatenate(
        [
            token_grads[:, 0].reshape(tokens, HEADS, HEAD_DIM),
            token_grads[:, 1].reshape(tokens, HEADS, HEAD_DIM),
        ],
        1,
    ).astype(jnp.float32)
    raw_grad = turn_back(rotated_grad)[0]
    proj_in_grad = jnp.concatenate([raw_grad, token_grads[:, 2].astype(jnp.float32)], 1).astype(
        jnp.bfloat16
    )
    qkv_grad = jnp.einsum("td,tf->df", normed_low, proj_in_grad, preferred_element_type=jnp.float32)
    normed_grad = jnp.einsum(
        "tf,df->td", proj_in_grad, qkv_full, preferred_element_type=jnp.float32
    )
    input_part, attn_gain_grad = norm_one_back(normed_grad)
    input_grad = (hidden_grad + input_part).astype(jnp.bfloat16)
    shares = (
        lax.psum_scatter(qkv_grad, "dp", scatter_dimension=0, tiled=True),
        lax.psum_scatter(proj_grad, "dp", scatter_dimension=0, tiled=True),
        lax.psum_scatter(in_grad, "dp", scatter_dimension=0, tiled=True),
        lax.psum_scatter(out_grad, "dp", scatter_dimension=0, tiled=True),
        lax.psum_scatter(attn_gain_grad, "dp", scatter_dimension=0, tiled=True),
        lax.psum_scatter(mlp_gain_grad, "dp", scatter_dimension=0, tiled=True),
    )
    totals = (
        lax.psum(shares[0].astype(jnp.bfloat16), "seq").astype(jnp.float32),
        lax.psum(shares[1].astype(jnp.bfloat16), "seq").astype(jnp.float32),
        lax.psum(shares[2].astype(jnp.bfloat16), "seq").astype(jnp.float32),
        lax.psum(shares[3].astype(jnp.bfloat16), "seq").astype(jnp.float32),
        lax.psum(shares[4].astype(jnp.bfloat16), "seq").astype(jnp.float32),
        lax.psum(shares[5].astype(jnp.bfloat16), "seq").astype(jnp.float32),
    )
    return (output, input_grad, totals[4], totals[0], totals[1], totals[5], totals[2], totals[3])


def solution(mesh):
    in_specs = (
        P(("dp", "seq"), None),
        P("dp"),
        P("dp", None),
        P("dp", None),
        P("dp"),
        P("dp", None),
        P("dp", None),
        P(("dp", "seq"), None),
    )
    out_specs = (
        P(("dp", "seq"), None),
        P(("dp", "seq"), None),
        P("dp"),
        P("dp", None),
        P("dp", None),
        P("dp"),
        P("dp", None),
        P("dp", None),
    )
    return jax.shard_map(shards, mesh=mesh, in_specs=in_specs, out_specs=out_specs, check_vma=False)
```

profile of v0, /device:TPU:0, one launch (start us, length us, event | category | flops | bytes accessed | tf_op | source)
XLA Modules:
  0.0 997.3 jit_solution(2272519886768296588)
XLA Ops:
  11.6 15.3 %all-reduce.11 = (bf16[768]{0:T(1024)(128)(2,1)S(1)}, bf16[768]{0:T(1024)(128)(2,1)S(1)}) all-reduce(bf16[768]{0:T(1024)(128)(2,1)S(1)} %dynamic-update-slice, bf16[768]{0:T(1024)(128)(2,1)S(1)} %dynamic-update-slice.1), channel_id=1, replica_groups=mesh['dp'=8,'seq'=4] {'dp'}, use_global_device_ids=true, to_apply=%add.6 | all-reduce | flops 1536 | bytes 6144
  29.0 17.7 %all-gather.5.cloned.1.call-done = bf16[768,2304]{1,0:T(8,128)(2,1)} async-done(((bf16[96,2304]{1,0:T(8,128)(2,1)}), bf16[768,2304]{1,0:T(8,128)(2,1)}) %all-gather.5.cloned.1.call-update) | async-done | bytes 3538960 | tf_op jit(solution)/shard_map/all_gather | solution.py:138
  46.7 6.2 fusion.81
  56.7 6.6 copy.55
  80.8 11.1 %copy.58 = bf16[1024,3,768]{0,1,2:T(4,128)(2,1)} copy(bf16[1024,3,768]{2,0,1:T(8,128)(2,1)} %pad_maximum_fusion) | data formatting | bytes 9437184 | tf_op jit(solution)/shard_map/stack | solution.py:165
  91.9 5.2 all-to-all-start
  98.6 137.3 %all-to-all-done = bf16[1024,3,768]{0,1,2:T(4,128)(2,1)} async-done(((bf16[1024,3,768]{0,1,2:T(4,128)(2,1)}), bf16[1024,3,768]{0,1,2:T(4,128)(2,1)}, u32[]{:S(2)}, u32[]{:S(2)}) %all-to-all-start) | async-done | bytes 4718624 | tf_op jit(solution)/shard_map/all_to_all | solution.py:166
  236.0 4.7 copy.59
  246.6 67.9 %while.30 = (s32[]{:T(128)}, bf16[8,512,3,64]{1,3,2,0:T(8,128)(2,1)}, f32[8,512,3]{1,2,0:T(4,128)}, s32[8]{0:T(128)S(1)}, bf16[4224,3,64]{0,2,1:T(8,128)(2,1)}, ...) while((s32[]{:T(128)}, ...), condition=%wide.region_5.6_spmd, body=%wide.region_2.5_spmd.sunk | while | flops 265094656 | bytes 14252788 | solution.py:77
  324.6 4.4 all-to-all-start.1
  332.6 33.3 %all-to-all-done.1 = bf16[4,1024,192]{1,2,0:T(8,128)(2,1)} async-done(((bf16[4,1024,192]{1,2,0:T(8,128)(2,1)}), bf16[4,1024,192]{1,2,0:T(8,128)(2,1)}, u32[]{:S(2)}, u32[]{:S(2)}) %all-to-all-start.1) | async-done | bytes 1572896 | tf_op jit(solution)/shard_map/all_to_all | solution.py:176
  371.3 10.7 %fusion.89 = f32[1024,2304]{1,0:T(8,128)} fusion(bf16[768,2304]{1,0:T(8,128)(2,1)} %all-gather.9.cloned.1.call-done, f32[1024,768]{0,1:T(8,128)} %copy-done.6, f32[768]{0:T(1024)S(1)} %convert_element_type.148, f32[1024]{0:T(1024)S(1)} %fusion.84, f32[1024]{0:T(1024)S(1)} %broadcast_multiply_fusion), kind=kOutput, calls=%fused_computation.152 | convolution fusion | flops 3627024384 | bytes 16133120 | tf_op jit(solution)/shard_map/dot_general | solution.py:181
  382.0 14.9 %fusion.76 = (f32[1024,1152]{1,0:T(8,128)}, f32[1024,1152]{1,0:T(8,128)S(1)}, f32[1024,1152]{1,0:T(8,128)S(1)}) fusion(f32[1024,2304]{1,0:T(8,128)} %fusion.89, bf16[1024,768]{1,0:T(8,128)(2,1)S(1)} %copy-done.15, bf16[1152,768]{1,0:T(8,128)(2,1)} %all-gather.11.cloned.1.call-done), kind=kOutput, calls=%fused_computation.125 | convolution fusion | flops 1888616448 | bytes 22216704 | tf_op jit(solution)/shard_map/td,fd->tf/dot_general | solution.py:188
  400.4 9.0 multiply_reduce_fusion.1
  413.0 4.3 fusion.98
  417.4 5.6 fusion.99
  432.0 11.4 %fusion.77 = f32[768,2304]{1,0:T(8,128)} fusion(f32[1024,1152]{1,0:T(8,128)} %copy-done.9, f32[1024,1152]{1,0:T(8,128)} %get-tuple-element.312, f32[1024,768]{0,1:T(8,128)} %copy-done.6, f32[768]{0:T(1024)S(1)} %convert_element_type.148, f32[1024]{0:T(1024)S(1)} %fusion.84, f32[1024]{0:T(1024)S(1)} %broadcast_multiply_fusion), kind=kOutput, calls=%fused_computation.126 | convolution fusion | flops 3631742976 | bytes 19672064 | tf_op jit(solution)/shard_map/td,tf->df/dot_general | solution.py:191
  443.5 24.9 %all-to-all-done.2 = bf16[1024,4,192]{0,2,1:T(8,128)(2,1)S(1)} async-done(((bf16[1024,4,192]{0,2,1:T(8,128)(2,1)}), bf16[1024,4,192]{0,2,1:T(8,128)(2,1)S(1)}, u32[]{:S(2)}, u32[]{:S(2)}) %all-to-all-start.2) | async-done | bytes 1572896 | tf_op jit(solution)/shard_map/all_to_all | solution.py:200
  479.1 134.9 %while.31 = (s32[]{:T(128)}, f32[4224,3,64]{0,2,1:T(8,128)}, f32[4224,3,64]{0,2,1:T(8,128)}, bf16[8,512,3,64]{1,3,2,0:T(8,128)(2,1)}, s32[8]{0:T(128)S(1)}, /*in...) while((s32[]{:T(128)}, f32[4224,3,64]{0,2,1:T(8,128)}, ...), condition=%wide.region_12.13_spmd, body=%wide.region_10.12_spmd.sunk | while | flops 640099840 | bytes 49803588 | solution.py:130
  518.7 4.2 multiply_reduce_fusion.5
  535.8 4.1 multiply_reduce_fusion.5
  624.4 12.8 %copy.67 = bf16[4096,3,192]{2,1,0:T(4,128)(2,1)} copy(bf16[4096,3,192]{0,2,1:T(8,128)(2,1)} %pad_maximum_fusion.1) | data formatting | bytes 9437184 | tf_op jit(solution)/shard_map/stack | solution.py:205
  637.2 190.6 %all_to_all.68 = bf16[4096,3,192]{2,1,0:T(4,128)(2,1)} all-to-all(bf16[4096,3,192]{2,1,0:T(4,128)(2,1)} %copy.67), channel_id=1, replica_groups=mesh['dp'=8,'seq'=4] {'seq'}, dimensions={0} | all-to-all | bytes 9437184 | tf_op jit(solution)/shard_map/all_to_all | solution.py:213
  827.8 12.8 %copy.69 = bf16[1024,3,4,192]{0,3,2,1:T(8,128)(2,1)} copy(bf16[1024,3,4,192]{3,1,0,2:T(4,128)(2,1)} %bitcast.117) | data formatting | bytes 9437184 | tf_op jit(solution)/shard_map/all_to_all | solution.py:213
  848.8 7.7 fusion.72
  857.2 6.7 add_convert_fusion.2
  870.4 8.6 fusion.71
  881.4 38.9 %reduce-scatter.5.cloned.1.call-done = f32[96,2304]{1,0:T(8,128)} async-done(((f32[768,2304]{1,0:T(8,128)}), f32[96,2304]{1,0:T(8,128)}) %reduce-scatter.5.cloned.1.call-update) | async-done | bytes 884752 | tf_op jit(solution)/shard_map/reduce_scatter | solution.py:232
  925.6 13.4 %all-reduce.10 = (bf16[768]{0:T(1024)(128)(2,1)S(1)}, bf16[768]{0:T(1024)(128)(2,1)S(1)}) all-reduce(f32[768]{0:T(1024)S(1)} %get-tuple-element.264, f32[768]{0:T(1024)S(1)} %get-tuple-element.262), channel_id=2, replica_groups=mesh['dp'=8,'seq'=4] {'dp'}, use_global_device_ids=true, to_apply=%region_16.17.clone | all-reduce | flops 1536 | bytes 9216
  939.1 12.3 %all-reduce.12 = (bf16[96]{0:T(256)(128)(2,1)S(1)}, bf16[96]{0:T(256)(128)(2,1)S(1)}) all-reduce(bf16[96]{0:T(256)(128)(2,1)S(1)} %dynamic-slice.9, bf16[96]{0:T(256)(128)(2,1)S(1)} %dynamic-slice.8), channel_id=1, replica_groups=mesh['dp'=8,'seq'=4] {'seq'}, use_global_device_ids=true, to_apply=%region_17.18 | all-reduce | flops 192 | bytes 768 | tf_op jit(solution)/shard_map/psum | solution.py:244
  952.4 5.5 add_convert_fusion.1
  960.5 23.2 %all-reduce.16.cloned.1.call-done = (bf16[96,2304]{1,0:T(8,128)(2,1)}, bf16[96,768]{1,0:T(8,128)(2,1)}, bf16[96,2304]{1,0:T(8,128)(2,1)}, bf16[144,768]{1,0:T(8,128)(2,1)}) async-done(((bf16[96,2304]{1,0:T(8,128)(2,1)}, bf16[96,768]{1,0:T(8,128)(2,1)}, bf16[96,2304]{1,0:T(8,128)(2,1)}, bf16[144,768]{1,0:T(8,128)(2,1)}), (bf16[96,2304]{1,0:T(8,128)(2,1)}, bf16[96,768]{1,0:T(8,128)(2,1)}, ...) | async-done | bytes 1253392 | tf_op jit(solution)/shard_map/psum | solution.py:240
  (347 shorter events, 307.2 us)
Async XLA Ops:
  7.2 4.1 copy-start.29
  7.2 39.5 %all-gather.5.cloned.1.call-start = ((), (), s32[]{:S(2)}) async-start(), calls=%async_computation.8 | async-start | bytes 3981312 | tf_op jit(solution)/shard_map/all_gather | solution.py:138
  9.7 356.2 %copy-start.1 = (bf16[1024,768]{0,1:T(8,128)(2,1)}, bf16[1024,768]{0,1:T(8,128)(2,1)S(1)}, u32[]{:S(2)}) copy-start(bf16[1024,768]{0,1:T(8,128)(2,1)S(1)} %copy.54) | copy-start | bytes 4718596
  26.9 26.0 %copy-start.21 = (f32[768]{0:T(1024)}, f32[768]{0:T(1024)S(1)}, u32[]{:S(2)}) copy-start(f32[768]{0:T(1024)S(1)} %convert_element_type.141) | copy-start | bytes 9220
  28.2 38.7 %copy-start.11 = (f32[1024,64]{0,1:T(8,128)}, f32[1024,64]{0,1:T(8,128)S(1)}, u32[]{:S(2)}) copy-start(f32[1024,64]{0,1:T(8,128)S(1)} %get-tuple-element.346) | copy-start | bytes 786436
  28.5 24.4 %copy-start.19 = (f32[1024]{0:T(1024)}, f32[1024]{0:T(1024)S(1)}, u32[]{:S(2)}) copy-start(f32[1024]{0:T(1024)S(1)} %broadcast_multiply_fusion.1) | copy-start | bytes 12292
  29.0 23.9 %copy-start.25 = (f32[1024]{0:T(1024)}, f32[1024]{0:T(1024)S(1)}, u32[]{:S(2)}) copy-start(f32[1024]{0:T(1024)S(1)} %fusion.70) | copy-start | bytes 12292
  29.0 23.9 %copy-start.23 = (f32[1024]{0:T(1024)}, f32[1024]{0:T(1024)S(1)}, u32[]{:S(2)}) copy-start(f32[1024]{0:T(1024)S(1)} %fusion.83) | copy-start | bytes 12292
  63.2 4.0 slice-start
  63.2 4.7 slice-start.1
  63.2 4.7 copy-start.13
  91.9 144.1 %all-to-all-start = ((bf16[1024,3,768]{0,1,2:T(4,128)(2,1)}), bf16[1024,3,768]{0,1,2:T(4,128)(2,1)}, u32[]{:S(2)}, u32[]{:S(2)}) async-start(bf16[1024,3,768]{0,1,2:T(4,128)(2,1)} %copy.58), calls=%async_computation | async-start | bytes 12582912 | tf_op jit(solution)/shard_map/all_to_all | solution.py:166
  97.1 235.5 %all-gather.7.cloned.1.call-start = ((), (), s32[]{:S(2)}) async-start(), calls=%async_computation.9 | async-start | bytes 1327104 | tf_op jit(solution)/shard_map/all_gather | solution.py:139
  97.9 273.4 %all-gather.9.cloned.1.call-start = ((), (), s32[]{:S(2)}) async-start(), calls=%async_computation.10 | async-start | bytes 3981312 | tf_op jit(solution)/shard_map/all_gather | solution.py:140
  324.6 41.3 %all-to-all-start.1 = ((bf16[4,1024,192]{1,2,0:T(8,128)(2,1)}), bf16[4,1024,192]{1,2,0:T(8,128)(2,1)}, u32[]{:S(2)}, u32[]{:S(2)}) async-start(bf16[4,1024,192]{1,2,0:T(8,128)(2,1)} %copy.62), calls=%async_computation.1 | async-start | bytes 3145728 | tf_op jit(solution)/shard_map/all_to_all | solution.py:176
  329.0 53.1 %all-gather.11.cloned.1.call-start = ((), (), s32[]{:S(2)}) async-start(), calls=%async_computation.11 | async-start | bytes 1990656 | tf_op jit(solution)/shard_map/all_gather | solution.py:141
  329.5 537.4 %reduce-scatter.7.cloned.1.call-start = ((), (), s32[]{:S(2)}) async-start(), calls=%async_computation.13 | async-start | bytes 2654208 | tf_op jit(solution)/shard_map/reduce_scatter | solution.py:233
  371.3 10.8 %copy-start.15 = (bf16[1024,768]{1,0:T(8,128)(2,1)S(1)}, bf16[1024,768]{1,0:T(8,128)(2,1)}, u32[]{:S(2)}) copy-start(bf16[1024,768]{1,0:T(8,128)(2,1)} %param.19) | copy-start | bytes 4718596
  382.0 14.9 %copy-start.8 = (f32[1024,2304]{1,0:T(8,128)S(1)}, f32[1024,2304]{1,0:T(8,128)}, u32[]{:S(2)}) copy-start(f32[1024,2304]{1,0:T(8,128)} %fusion.89) | copy-start | bytes 28311556
  400.4 9.0 copy-start.9
  417.3 451.3 %reduce-scatter.11.cloned.1.call-start = ((), (), s32[]{:S(2)}) async-start(), calls=%async_computation.15 | async-start | bytes 3981312 | tf_op jit(solution)/shard_map/reduce_scatter | solution.py:235
  428.4 40.0 %all-to-all-start.2 = ((bf16[1024,4,192]{0,2,1:T(8,128)(2,1)}), bf16[1024,4,192]{0,2,1:T(8,128)(2,1)S(1)}, u32[]{:S(2)}, u32[]{:S(2)}) async-start(bf16[1024,4,192]{0,2,1:T(8,128)(2,1)} %bitcast.135), calls=%async_computation.2 | async-start | bytes 3145728 | tf_op jit(solution)/shard_map/all_to_all | solution.py:200
  431.9 447.2 %reduce-scatter.9.cloned.1.call-start = ((), (), s32[]{:S(2)}) async-start(), calls=%async_computation.14 | async-start | bytes 7962624 | tf_op jit(solution)/shard_map/reduce_scatter | solution.py:234
  443.4 476.9 %reduce-scatter.5.cloned.1.call-start = ((), (), s32[]{:S(2)}) async-start(), calls=%async_computation.12 | async-start | bytes 7962624 | tf_op jit(solution)/shard_map/reduce_scatter | solution.py:232
  502.0 4.0 copy-start
  518.7 4.2 copy-start
  535.8 4.5 copy-start
  569.8 4.0 copy-start
  856.5 127.2 %all-reduce.16.cloned.1.call-start = ((), (), s32[]{:S(2)}) async-start(), calls=%async_computation.16 | async-start | bytes 2506752 | tf_op jit(solution)/shard_map/psum | solution.py:240
  870.4 8.6 copy-start.26
  922.3 30.1 %copy-start.5 = (bf16[1024,768]{0,1:T(8,128)(2,1)S(1)}, bf16[1024,768]{0,1:T(8,128)(2,1)}, u32[]{:S(2)}) copy-start(bf16[1024,768]{0,1:T(8,128)(2,1)} %copy.64) | copy-start | bytes 4718596
  983.8 5.7 copy-start.18
  (19 other events, 52.0 us)
Sparse Core Ops, SparseCore 0:
  9.9 36.7 all-gather.4
  99.8 24.4 all-gather.6
  126.3 33.9 all-gather.8
  331.4 26.9 all-gather.10
  417.5 40.6 reduce-scatter.6
  461.8 48.0 reduce-scatter.10
  513.9 65.5 reduce-scatter.8
  856.7 63.5 reduce-scatter.4
  923.7 59.9 all-reduce.15
where the time goes:
time: 1010 us; the launch traced here: 997 us
  waiting for transfers between devices  278 us (28%)
  matrix products  244 us (24%)
  blocking collectives  232 us (23%)
  local copies, waits for them, and re-layouts  131 us (13%)
  other arithmetic  72 us (7%)
  between operations  16.2 us (2%)
  starting transfers between devices  14.1 us (1%)
  loops' own time  10.6 us (1%)
    all_to_all x1, blocking collectives, shards(): lax.all_to_all(head_grads, 'seq', split_axis=0, concat_axis=2, tiled=True)  191 us
    all_to_all x1, waiting for transfers between devices, shards(): lax.all_to_all(stacked, 'seq', split_axis=2, concat_axis=0, tiled=True)  137 us
    dot_general x16, matrix products, band_scores(): jnp.einsum('qhd,khd->hqk', query_block, key_block, preferred_element_type...  48.2 us
    reduce_scatter x1, waiting for transfers between devices, shards(): lax.psum_scatter(qkv_grad, 'dp', scatter_dimension=0, tiled=True)  38.9 us
    all_to_all x1, waiting for transfers between devices, shards(): lax.all_to_all(attended_low, 'seq', split_axis=0, concat_axis=1, tiled=True)  33.3 us
    unnamed x2, blocking collectives  28.7 us
    dot_general x8, matrix products, one_block(): jnp.einsum('qhd,khd->hqk', grad_block, value_block, preferred_element_typ...  28.3 us
    dot_general x8, matrix products, one_block(): jnp.einsum('hqk,khd->qhd', softmax_low, value_block, preferred_element_ty...  25.1 us
  transfers between devices with their start and end apart: 12, of which 6 were waited for; matrix products, arithmetic and copies ran while one was open for 35% of the time, Pallas kernels for 0%

commit v1 on v0

--- a/solution.py
+++ b/solution.py
@@ -210,7 +210,20 @@
         ],
         1,
     ).astype(jnp.bfloat16)
-    token_grads = lax.all_to_all(head_grads, "seq", split_axis=0, concat_axis=2, tiled=True)
+    ways, here = (lax.axis_size("seq"), lax.axis_index("seq"))
+    width = head_grads.shape[0] // ways
+    shape = list(head_grads.shape)
+    shape[0] = width
+    height = shape[2]
+    shape[2] = height * ways
+    token_grads = jnp.zeros(shape, head_grads.dtype)
+    for mask in range(ways):
+        part = lax.dynamic_slice_in_dim(head_grads, (here ^ mask) * width, width, axis=0)
+        if mask:
+            part = lax.ppermute(part, "seq", [(d, d ^ mask) for d in range(ways)])
+        token_grads = lax.dynamic_update_slice_in_dim(
+            token_grads, part, (here ^ mask) * height, axis=2
+        )
     rotated_grad = jnp.concatenate(
         [
             token_grads[:, 0].reshape(tokens, HEADS, HEAD_DIM),

time: 1010 us -> 899 us (0.89)
  blocking collectives: 232 us -> 41 us
  waiting for transfers between devices: 278 us -> 375 us
  local copies, waits for them, and re-layouts: 131 us -> 113 us
    all_to_all x1 -> x0, blocking collectives: 191 us -> none  [shards(): lax.all_to_all(head_grads, 'seq', split_axis=0, concat_axis=2, tiled=True)]
    ppermute x0 -> x3, waiting for transfers between devices: none -> 75.1 us  [shards(): part = lax.ppermute(part, 'seq', [(d, d ^ mask) for d in range(ways)])]
    reduce_scatter x1, waiting for transfers between devices: 38.9 us -> 61.4 us  [shards(): lax.psum_scatter(qkv_grad, 'dp', scatter_dimension=0, tiled=True)]
    another operation x2 -> x1, local copies, waits for them, and re-layouts: 13.6 us -> 0.78 us  [shards(): jnp.stack([query_grad.reshape(seq_total, D // seq_count), key_pad_grad[WI...]
    all_to_all x1 -> x0, local copies, waits for them, and re-layouts: 12.8 us -> none  [shards(): lax.all_to_all(head_grads, 'seq', split_axis=0, concat_axis=2, tiled=True)]
  transfers between devices with their start and end apart: 12 -> 15, of which waited for: 6 -> 8; matrix products, arithmetic and copies ran while one was open for 35% -> 38% of each run, Pallas kernels for 0% -> 0%
where the time goes in v1:
time: 899 us; the launch traced here: 888 us
  waiting for transfers between devices  375 us (42%)
  matrix products  245 us (27%)
  local copies, waits for them, and re-layouts  113 us (13%)
  other arithmetic  69.6 us (8%)
  blocking collectives  41 us (5%)
  starting transfers between devices  18.5 us (2%)
  between operations  16.2 us (2%)
  loops' own time  9.62 us (1%)
    all_to_all x1, waiting for transfers between devices, shards(): lax.all_to_all(stacked, 'seq', split_axis=2, concat_axis=0, tiled=True)  137 us
    ppermute x3, waiting for transfers between devices, shards(): part = lax.ppermute(part, 'seq', [(d, d ^ mask) for d in range(ways)])  75.1 us
    reduce_scatter x1, waiting for transfers between devices, shards(): lax.psum_scatter(qkv_grad, 'dp', scatter_dimension=0, tiled=True)  61.4 us
    dot_general x16, matrix products, band_scores(): jnp.einsum('qhd,khd->hqk', query_block, key_block, preferred_element_type...  48.6 us
    all_to_all x1, waiting for transfers between devices, shards(): lax.all_to_all(attended_low, 'seq', split_axis=0, concat_axis=1, tiled=True)  33.3 us
    dot_general x8, matrix products, one_block(): jnp.einsum('qhd,khd->hqk', grad_block, value_block, preferred_element_typ...  28.9 us
    unnamed x2, blocking collectives  28.7 us
    dot_general x8, matrix products, one_block(): jnp.einsum('hqk,khd->qhd', softmax_low, value_block, preferred_element_ty...  25.1 us
  transfers between devices with their start and end apart: 15, of which 8 were waited for; matrix products, arithmetic and copies ran while one was open for 38% of the time, Pallas kernels for 0%

profile of v1, /device:TPU:0, one launch (start us, length us, event | category | flops | bytes accessed | tf_op | source)
XLA Modules:
  0.0 888.0 jit_solution(9546111749362094757)
XLA Ops:
  11.5 15.3 %all-reduce.11 = (bf16[768]{0:T(1024)(128)(2,1)S(1)}, bf16[768]{0:T(1024)(128)(2,1)S(1)}) all-reduce(bf16[768]{0:T(1024)(128)(2,1)S(1)} %dynamic-update-slice, bf16[768]{0:T(1024)(128)(2,1)S(1)} %dynamic-update-slice.1), channel_id=1, replica_groups=mesh['dp'=8,'seq'=4] {'dp'}, use_global_device_ids=true, to_apply=%add.6 | all-reduce | flops 1536 | bytes 6144
  29.0 17.7 %all-gather.5.cloned.1.call-done = bf16[768,2304]{1,0:T(8,128)(2,1)} async-done(((bf16[96,2304]{1,0:T(8,128)(2,1)}), bf16[768,2304]{1,0:T(8,128)(2,1)}) %all-gather.5.cloned.1.call-update) | async-done | bytes 3538960 | tf_op jit(solution)/shard_map/all_gather | solution.py:138
  46.7 6.2 fusion.81
  56.7 6.6 copy.41
  80.7 11.1 %copy.44 = bf16[1024,3,768]{0,1,2:T(4,128)(2,1)} copy(bf16[1024,3,768]{2,0,1:T(8,128)(2,1)} %pad_maximum_fusion) | data formatting | bytes 9437184 | tf_op jit(solution)/shard_map/stack | solution.py:165
  91.8 5.3 all-to-all-start
  98.6 137.3 %all-to-all-done = bf16[1024,3,768]{0,1,2:T(4,128)(2,1)} async-done(((bf16[1024,3,768]{0,1,2:T(4,128)(2,1)}), bf16[1024,3,768]{0,1,2:T(4,128)(2,1)}, u32[]{:S(2)}, u32[]{:S(2)}) %all-to-all-start) | async-done | bytes 4718624 | tf_op jit(solution)/shard_map/all_to_all | solution.py:166
  235.9 4.7 copy.45
  246.6 67.9 %while.30 = (s32[]{:T(128)}, bf16[8,512,3,64]{1,3,2,0:T(8,128)(2,1)}, f32[8,512,3]{1,2,0:T(4,128)}, s32[8]{0:T(128)S(1)}, bf16[4224,3,64]{0,2,1:T(8,128)(2,1)}, ...) while((s32[]{:T(128)}, ...), condition=%wide.region_5.6_spmd, body=%wide.region_2.5_spmd.sunk | while | flops 265094656 | bytes 14252788 | solution.py:77
  324.6 4.3 all-to-all-start.1
  332.6 33.3 %all-to-all-done.1 = bf16[4,1024,192]{1,2,0:T(8,128)(2,1)} async-done(((bf16[4,1024,192]{1,2,0:T(8,128)(2,1)}), bf16[4,1024,192]{1,2,0:T(8,128)(2,1)}, u32[]{:S(2)}, u32[]{:S(2)}) %all-to-all-start.1) | async-done | bytes 1572896 | tf_op jit(solution)/shard_map/all_to_all | solution.py:176
  371.3 10.7 %fusion.89 = f32[1024,2304]{1,0:T(8,128)} fusion(bf16[768,2304]{1,0:T(8,128)(2,1)} %all-gather.9.cloned.1.call-done, f32[1024,768]{0,1:T(8,128)} %copy-done.6, f32[768]{0:T(1024)S(1)} %convert_element_type.148, f32[1024]{0:T(1024)S(1)} %fusion.84, f32[1024]{0:T(1024)S(1)} %broadcast_multiply_fusion), kind=kOutput, calls=%fused_computation.159 | convolution fusion | flops 3627024384 | bytes 16133120 | tf_op jit(solution)/shard_map/dot_general | solution.py:181
  382.0 14.9 %fusion.76 = (f32[1024,1152]{1,0:T(8,128)}, f32[1024,1152]{1,0:T(8,128)S(1)}, f32[1024,1152]{1,0:T(8,128)S(1)}) fusion(f32[1024,2304]{1,0:T(8,128)} %fusion.89, bf16[1024,768]{1,0:T(8,128)(2,1)S(1)} %copy-done.15, bf16[1152,768]{1,0:T(8,128)(2,1)} %all-gather.11.cloned.1.call-done), kind=kOutput, calls=%fused_computation.125 | convolution fusion | flops 1888616448 | bytes 22216704 | tf_op jit(solution)/shard_map/td,fd->tf/dot_general | solution.py:188
  400.5 9.0 %multiply_reduce_fusion.1 = (f32[768]{0:T(1024)S(1)}, f32[1024]{0:T(1024)S(1)}, f32[1024,768]{0,1:T(8,128)S(1)}) fusion(f32[1024,768]{0,1:T(8,128)S(1)} %copy-done.7, f32[1024]{0:T(1024)S(1)} %fusion.84, f32[1024]{0:T(1024)S(1)} %broadcast_multiply_fusion, f32[768]{0:T(1024)S(1)} %convert_element_type.148, ...), kind=kOutput, calls=%fused_computation.112 | convolution fusion | flops 3634100480 | bytes 19286016 | tf_op jit(solution)/shard_map/tf,df->td/dot_general | solution.py:192
  413.2 4.3 fusion.98
  417.6 5.5 fusion.99
  432.1 11.5 %fusion.77 = f32[768,2304]{1,0:T(8,128)} fusion(f32[1024,1152]{1,0:T(8,128)} %copy-done.9, f32[1024,1152]{1,0:T(8,128)} %get-tuple-element.304, f32[1024,768]{0,1:T(8,128)} %copy-done.6, f32[768]{0:T(1024)S(1)} %convert_element_type.148, f32[1024]{0:T(1024)S(1)} %fusion.84, f32[1024]{0:T(1024)S(1)} %broadcast_multiply_fusion), kind=kOutput, calls=%fused_computation.127 | convolution fusion | flops 3631742976 | bytes 19672064 | tf_op jit(solution)/shard_map/td,tf->df/dot_general | solution.py:191
  443.6 24.8 %all-to-all-done.2 = bf16[1024,4,192]{0,2,1:T(8,128)(2,1)S(1)} async-done(((bf16[1024,4,192]{0,2,1:T(8,128)(2,1)}), bf16[1024,4,192]{0,2,1:T(8,128)(2,1)S(1)}, u32[]{:S(2)}, u32[]{:S(2)}) %all-to-all-start.2) | async-done | bytes 1572896 | tf_op jit(solution)/shard_map/all_to_all | solution.py:200
  479.0 134.3 %while.31 = (s32[]{:T(128)}, f32[4224,3,64]{0,2,1:T(8,128)}, f32[4224,3,64]{0,2,1:T(8,128)}, bf16[8,512,3,64]{1,3,2,0:T(8,128)(2,1)}, s32[8]{0:T(128)S(1)}, /*in...) while((s32[]{:T(128)}, f32[4224,3,64]{0,2,1:T(8,128)}, ...), condition=%wide.region_12.13_spmd, body=%wide.region_10.12_spmd.sunk | while | flops 640099840 | bytes 49803588 | solution.py:130
  501.6 4.1 multiply_reduce_fusion.5
  518.3 4.6 multiply_reduce_fusion.5
  602.7 4.0 multiply_reduce_fusion.5
  631.3 47.7 %collective-permute-done = bf16[1024,3,192]{0,2,1:T(8,128)(2,1)S(1)} collective-permute-done((bf16[1024,3,192]{0,2,1:T(8,128)(2,1)}, bf16[1024,3,192]{0,2,1:T(8,128)(2,1)S(1)}, u32[]{:S(2)}, u32[]{:S(2)}) %collective-permute-start) | collective-permute-done | bytes 1179680 | tf_op jit(solution)/shard_map/ppermute | solution.py:223
  680.0 27.4 %collective-permute-done.1 = bf16[1024,3,192]{0,2,1:T(8,128)(2,1)S(1)} collective-permute-done((bf16[1024,3,192]{0,2,1:T(8,128)(2,1)}, bf16[1024,3,192]{0,2,1:T(8,128)(2,1)S(1)}, u32[]{:S(2)}, u32[]{:S(2)}) %collective-permute-start.1) | collective-permute-done | bytes 1179680 | tf_op jit(solution)/shard_map/ppermute | solution.py:223
  717.9 8.0 fusion.72
  726.6 6.5 add_convert_fusion.2
  737.4 8.5 fusion.71
  749.7 61.4 %reduce-scatter.5.cloned.1.call-done = f32[96,2304]{1,0:T(8,128)} async-done(((f32[768,2304]{1,0:T(8,128)}), f32[96,2304]{1,0:T(8,128)}) %reduce-scatter.5.cloned.1.call-update) | async-done | bytes 884752 | tf_op jit(solution)/shard_map/reduce_scatter | solution.py:245
  816.3 13.4 %all-reduce.10 = (bf16[768]{0:T(1024)(128)(2,1)S(1)}, bf16[768]{0:T(1024)(128)(2,1)S(1)}) all-reduce(f32[768]{0:T(1024)S(1)} %get-tuple-element.256, f32[768]{0:T(1024)S(1)} %get-tuple-element.254), channel_id=2, replica_groups=mesh['dp'=8,'seq'=4] {'dp'}, use_global_device_ids=true, to_apply=%region_16.17.clone | all-reduce | flops 1536 | bytes 9216
  829.8 12.3 %all-reduce.12 = (bf16[96]{0:T(256)(128)(2,1)S(1)}, bf16[96]{0:T(256)(128)(2,1)S(1)}) all-reduce(bf16[96]{0:T(256)(128)(2,1)S(1)} %dynamic-slice.9, bf16[96]{0:T(256)(128)(2,1)S(1)} %dynamic-slice.8), channel_id=1, replica_groups=mesh['dp'=8,'seq'=4] {'seq'}, use_global_device_ids=true, to_apply=%region_17.18 | all-reduce | flops 192 | bytes 768 | tf_op jit(solution)/shard_map/psum | solution.py:257
  843.2 5.5 add_convert_fusion.1
  851.2 23.3 %all-reduce.16.cloned.1.call-done = (bf16[96,2304]{1,0:T(8,128)(2,1)}, bf16[96,768]{1,0:T(8,128)(2,1)}, bf16[96,2304]{1,0:T(8,128)(2,1)}, bf16[144,768]{1,0:T(8,128)(2,1)}) async-done(((bf16[96,2304]{1,0:T(8,128)(2,1)}, bf16[96,768]{1,0:T(8,128)(2,1)}, bf16[96,2304]{1,0:T(8,128)(2,1)}, bf16[144,768]{1,0:T(8,128)(2,1)}), (bf16[96,2304]{1,0:T(8,128)(2,1)}, bf16[96,768]{1,0:T(8,128)(2,1)}, ...) | async-done | bytes 1253392 | tf_op jit(solution)/shard_map/psum | solution.py:253
  (355 shorter events, 313.1 us)
Async XLA Ops:
  7.2 4.1 copy-start.29
  7.2 39.5 %all-gather.5.cloned.1.call-start = ((), (), s32[]{:S(2)}) async-start(), calls=%async_computation.7 | async-start | bytes 3981312 | tf_op jit(solution)/shard_map/all_gather | solution.py:138
  9.7 356.2 %copy-start.1 = (bf16[1024,768]{0,1:T(8,128)(2,1)}, bf16[1024,768]{0,1:T(8,128)(2,1)S(1)}, u32[]{:S(2)}) copy-start(bf16[1024,768]{0,1:T(8,128)(2,1)S(1)} %copy.40) | copy-start | bytes 4718596
  26.9 26.0 %copy-start.21 = (f32[768]{0:T(1024)}, f32[768]{0:T(1024)S(1)}, u32[]{:S(2)}) copy-start(f32[768]{0:T(1024)S(1)} %convert_element_type.141) | copy-start | bytes 9220
  28.2 38.7 %copy-start.11 = (f32[1024,64]{0,1:T(8,128)}, f32[1024,64]{0,1:T(8,128)S(1)}, u32[]{:S(2)}) copy-start(f32[1024,64]{0,1:T(8,128)S(1)} %get-tuple-element.342) | copy-start | bytes 786436
  28.5 24.4 %copy-start.19 = (f32[1024]{0:T(1024)}, f32[1024]{0:T(1024)S(1)}, u32[]{:S(2)}) copy-start(f32[1024]{0:T(1024)S(1)} %broadcast_multiply_fusion.1) | copy-start | bytes 12292
  29.0 23.9 %copy-start.25 = (f32[1024]{0:T(1024)}, f32[1024]{0:T(1024)S(1)}, u32[]{:S(2)}) copy-start(f32[1024]{0:T(1024)S(1)} %fusion.70) | copy-start | bytes 12292
  29.0 23.9 %copy-start.23 = (f32[1024]{0:T(1024)}, f32[1024]{0:T(1024)S(1)}, u32[]{:S(2)}) copy-start(f32[1024]{0:T(1024)S(1)} %fusion.83) | copy-start | bytes 12292
  63.3 4.7 slice-start.1
  63.3 4.7 copy-start.13
  91.8 144.1 %all-to-all-start = ((bf16[1024,3,768]{0,1,2:T(4,128)(2,1)}), bf16[1024,3,768]{0,1,2:T(4,128)(2,1)}, u32[]{:S(2)}, u32[]{:S(2)}) async-start(bf16[1024,3,768]{0,1,2:T(4,128)(2,1)} %copy.44), calls=%async_computation | async-start | bytes 12582912 | tf_op jit(solution)/shard_map/all_to_all | solution.py:166
  97.1 235.5 %all-gather.7.cloned.1.call-start = ((), (), s32[]{:S(2)}) async-start(), calls=%async_computation.8 | async-start | bytes 1327104 | tf_op jit(solution)/shard_map/all_gather | solution.py:139
  97.8 273.4 %all-gather.9.cloned.1.call-start = ((), (), s32[]{:S(2)}) async-start(), calls=%async_computation.9 | async-start | bytes 3981312 | tf_op jit(solution)/shard_map/all_gather | solution.py:140
  324.6 41.3 %all-to-all-start.1 = ((bf16[4,1024,192]{1,2,0:T(8,128)(2,1)}), bf16[4,1024,192]{1,2,0:T(8,128)(2,1)}, u32[]{:S(2)}, u32[]{:S(2)}) async-start(bf16[4,1024,192]{1,2,0:T(8,128)(2,1)} %copy.48), calls=%async_computation.1 | async-start | bytes 3145728 | tf_op jit(solution)/shard_map/all_to_all | solution.py:176
  329.0 53.0 %all-gather.11.cloned.1.call-start = ((), (), s32[]{:S(2)}) async-start(), calls=%async_computation.10 | async-start | bytes 1990656 | tf_op jit(solution)/shard_map/all_gather | solution.py:141
  329.5 406.2 %reduce-scatter.7.cloned.1.call-start = ((), (), s32[]{:S(2)}) async-start(), calls=%async_computation.12 | async-start | bytes 2654208 | tf_op jit(solution)/shard_map/reduce_scatter | solution.py:246
  371.2 10.8 %copy-start.15 = (bf16[1024,768]{1,0:T(8,128)(2,1)S(1)}, bf16[1024,768]{1,0:T(8,128)(2,1)}, u32[]{:S(2)}) copy-start(bf16[1024,768]{1,0:T(8,128)(2,1)} %param.19) | copy-start | bytes 4718596
  382.0 15.0 %copy-start.8 = (f32[1024,2304]{1,0:T(8,128)S(1)}, f32[1024,2304]{1,0:T(8,128)}, u32[]{:S(2)}) copy-start(f32[1024,2304]{1,0:T(8,128)} %fusion.89) | copy-start | bytes 28311556
  400.5 9.0 %copy-start.9 = (f32[1024,1152]{1,0:T(8,128)}, f32[1024,1152]{1,0:T(8,128)S(1)}, u32[]{:S(2)}) copy-start(f32[1024,1152]{1,0:T(8,128)S(1)} %get-tuple-element.314) | copy-start | bytes 14155780
  417.5 328.4 %reduce-scatter.11.cloned.1.call-start = ((), (), s32[]{:S(2)}) async-start(), calls=%async_computation.14 | async-start | bytes 3981312 | tf_op jit(solution)/shard_map/reduce_scatter | solution.py:248
  428.4 39.9 %all-to-all-start.2 = ((bf16[1024,4,192]{0,2,1:T(8,128)(2,1)}), bf16[1024,4,192]{0,2,1:T(8,128)(2,1)S(1)}, u32[]{:S(2)}, u32[]{:S(2)}) async-start(bf16[1024,4,192]{0,2,1:T(8,128)(2,1)} %bitcast.128), calls=%async_computation.2 | async-start | bytes 3145728 | tf_op jit(solution)/shard_map/all_to_all | solution.py:200
  432.0 315.7 %reduce-scatter.9.cloned.1.call-start = ((), (), s32[]{:S(2)}) async-start(), calls=%async_computation.13 | async-start | bytes 7962624 | tf_op jit(solution)/shard_map/reduce_scatter | solution.py:247
  443.6 367.5 %reduce-scatter.5.cloned.1.call-start = ((), (), s32[]{:S(2)}) async-start(), calls=%async_computation.11 | async-start | bytes 7962624 | tf_op jit(solution)/shard_map/reduce_scatter | solution.py:245
  518.3 4.6 copy-start
  535.8 4.3 copy-start
  626.9 52.1 %collective-permute-start = (bf16[1024,3,192]{0,2,1:T(8,128)(2,1)}, bf16[1024,3,192]{0,2,1:T(8,128)(2,1)S(1)}, u32[]{:S(2)}, u32[]{:S(2)}) collective-permute-start(bf16[1024,3,192]{0,2,1:T(8,128)(2,1)} %get-tuple-element.325), channel_id=1, source_target_pairs={{0,1},{1,0},{2,3},{3,2},{4,5},{5,4},{6,7},{7,6},{8,9},{9,8},{10,11... | collective-permute-start | bytes 3538952 | tf_op jit(solution)/shard_map/ppermute | solution.py:223
  626.9 80.6 %collective-permute-start.1 = (bf16[1024,3,192]{0,2,1:T(8,128)(2,1)}, bf16[1024,3,192]{0,2,1:T(8,128)(2,1)S(1)}, u32[]{:S(2)}, u32[]{:S(2)}) collective-permute-start(bf16[1024,3,192]{0,2,1:T(8,128)(2,1)} %get-tuple-element.324), channel_id=1, source_target_pairs={{0,2},{1,3},{2,0},{3,1},{4,6},{5,7},{6,4},{7,5},{8,10},{9,11},{10,... | collective-permute-start | bytes 3538952 | tf_op jit(solution)/shard_map/ppermute | solution.py:223
  628.9 79.7 %collective-permute-start.2 = (bf16[1024,3,192]{0,2,1:T(8,128)(2,1)}, bf16[1024,3,192]{0,2,1:T(8,128)(2,1)S(1)}, u32[]{:S(2)}, u32[]{:S(2)}) collective-permute-start(bf16[1024,3,192]{0,2,1:T(8,128)(2,1)} %get-tuple-element.323), channel_id=1, source_target_pairs={{0,3},{1,2},{2,1},{3,0},{4,7},{5,6},{6,5},{7,4},{8,11},{9,10},{10,... | collective-permute-start | bytes 3538952 | tf_op jit(solution)/shard_map/ppermute | solution.py:223
  725.9 148.6 %all-reduce.16.cloned.1.call-start = ((), (), s32[]{:S(2)}) async-start(), calls=%async_computation.15 | async-start | bytes 2506752 | tf_op jit(solution)/shard_map/psum | solution.py:253
  737.4 8.5 copy-start.26
  813.0 30.1 %copy-start.5 = (bf16[1024,768]{0,1:T(8,128)(2,1)S(1)}, bf16[1024,768]{0,1:T(8,128)(2,1)}, u32[]{:S(2)}) copy-start(bf16[1024,768]{0,1:T(8,128)(2,1)} %copy.50) | copy-start | bytes 4718596
  874.5 5.7 copy-start.18
  (22 other events, 64.1 us)
Sparse Core Ops, SparseCore 0:
  9.9 36.7 all-gather.4
  99.8 24.4 all-gather.6
  126.2 33.9 all-gather.8
  331.4 26.9 all-gather.10
  417.6 40.6 reduce-scatter.6
  462.0 48.0 reduce-scatter.10
  514.1 65.5 reduce-scatter.8
  726.0 84.9 reduce-scatter.4
  814.5 59.9 all-reduce.15
